TPU v7x, 32 devices: a whole 2x2x4 slice. The times are simulated.
32 devices in a mesh: dom: 8 (over z, y), feat: 4 (over x, core).
Axes of the slice: x: 2, y: 2, z: 4, core: 2. Of those that a mesh axis runs over, the one named last changes fastest.
Arguments:
- features: bfloat16 [32768, 512], P('dom', 'feat'), may hold values from -6 to 6
- theta: bfloat16 [512, 512], P(None, 'feat'), may hold values from -0.25 to 0.25
- incidence: int32 [3, 4096], P(None, 'dom'), may hold values from 0 to 4095, as said below
- edge_weight: float32 [16384], P('dom'), may hold values from 0.5 to 2
- cotangent: bfloat16 [32768, 512], P('dom', 'feat'), may hold values from -6 to 6
Outputs:
- activation: bfloat16 [32768, 512], P('dom', 'feat')
- grad_features: bfloat16 [32768, 512], P('dom', 'feat')
- grad_theta: float32 [512, 512], P('dom', 'feat')
Inputs may be any that keep to these rules, and one draw needn't show every extreme that they name: `incidence`: in the 64 slots from one vertex owner to one hyperedge owner the live slots (weight over zero) come first, at least one of them; some hyperedge owner receives all 64 slots live from every vertex owner.
All inputs are finite; a program needn't handle non-finite values.
Results may differ from a plain program's by a relative error of at most 0.0073.
Values may be sent and summed in bfloat16 or wider, within the bound.
A program may use at most 64 MiB of HBM per device.

v0:
```python
import jax
import jax.numpy as jnp
from jax import lax
from jax.sharding import PartitionSpec as P


def local(features, theta, incidence, edge_weight, cotangent):
    owners = lax.axis_size("dom")
    nvert = features.shape[0]
    cols = features.shape[1]
    nedge = edge_weight.shape[0]
    vert = incidence[0]
    edge = incidence[1]
    weight = incidence[2]
    weight_f = weight.astype(jnp.float32)
    dvis = lax.rsqrt(1.0 + jax.ops.segment_sum(weight_f, vert, num_segments=nvert))
    slot_scale = weight_f * dvis[vert]
    full_rows = lax.all_gather(features, "feat", axis=1, tiled=True)
    projected = jnp.dot(full_rows, theta, preferred_element_type=jnp.float32).astype(jnp.bfloat16)
    message = (slot_scale[:, None] * projected[vert].astype(jnp.float32)).astype(jnp.bfloat16)
    recv_rows, recv_edge, recv_weight = (
        lax.all_to_all(
            message.reshape(owners, -1, cols), "dom", split_axis=0, concat_axis=0, tiled=True
        ),
        lax.all_to_all(edge.reshape(owners, -1), "dom", split_axis=0, concat_axis=0, tiled=True),
        lax.all_to_all(weight.reshape(owners, -1), "dom", split_axis=0, concat_axis=0, tiled=True),
    )
    recv_edge = recv_edge.reshape(-1)
    degree = 1.0 + jax.ops.segment_sum(
        recv_weight.reshape(-1).astype(jnp.float32), recv_edge, num_segments=nedge
    )
    edge_scale = edge_weight / degree

    def edge_side(rows):
        edge_sum = jax.ops.segment_sum(
            rows.reshape(-1, cols).astype(jnp.float32), recv_edge, num_segments=nedge
        )
        edge_rows = (edge_scale[:, None] * edge_sum).astype(jnp.bfloat16)
        return edge_rows[recv_edge].reshape(owners, -1, cols)

    def vertex_side(back):
        terms = weight_f[:, None] * back.reshape(-1, cols).astype(jnp.float32)
        return dvis[:, None] * jax.ops.segment_sum(terms, vert, num_segments=nvert)

    back = lax.all_to_all(edge_side(recv_rows), "dom", split_axis=0, concat_axis=0, tiled=True)
    summed = vertex_side(back)
    sigma = jax.nn.sigmoid(summed)
    activation = (summed * sigma).astype(jnp.bfloat16)
    slope = sigma * (1.0 + summed * (1.0 - sigma))
    grad_summed = cotangent.astype(jnp.float32) * slope
    grad_message = (slot_scale[:, None] * grad_summed[vert]).astype(jnp.bfloat16)
    grad_recv = lax.all_to_all(
        grad_message.reshape(owners, -1, cols), "dom", split_axis=0, concat_axis=0, tiled=True
    )
    grad_back = lax.all_to_all(edge_side(grad_recv), "dom", split_axis=0, concat_axis=0, tiled=True)
    grad_projected = vertex_side(grad_back).astype(jnp.bfloat16)
    theta_full = lax.all_gather(theta, "feat", axis=1, tiled=True)
    theta_mine = lax.dynamic_slice_in_dim(theta_full, lax.axis_index("feat") * cols, cols, 0)
    grad_total = lax.dot_general(
        lax.all_gather(grad_projected, "feat", axis=1, tiled=True),
        theta_mine,
        (((1,), (1,)), ((), ())),
        preferred_element_type=jnp.float32,
    )
    grad_features = grad_total.astype(jnp.bfloat16)
    share = full_rows.shape[1] // owners
    term = lax.dot_general(
        full_rows, grad_projected, (((0,), (0,)), ((), ())), preferred_element_type=jnp.float32
    )
    total = lax.psum(term, "dom")
    grad_theta = lax.dynamic_slice_in_dim(total, lax.axis_index("dom") * share, share, 0)
    return (activation, grad_features, grad_theta)


def solution(mesh):
    placed = (P("dom", "feat"), P(None, "feat"), P(None, "dom"), P("dom"), P("dom", "feat"))
    return jax.shard_map(
        local,
        mesh=mesh,
        in_specs=placed,
        out_specs=(P("dom", "feat"), P("dom", "feat"), P("dom", "feat")),
        check_vma=False,
    )
```

profile of v0, /device:TPU:0, one launch (start us, length us, event | category | flops | bytes accessed | tf_op | source)
XLA Modules:
  0.0 234.5 jit_solution(12169646869658793668)
XLA Ops:
  9.4 7.3 %all-to-all-start = ((s32[8,1,64]{2,1,0:T(1,128)}), s32[8,1,64]{2,1,0:T(1,128)S(1)}, u32[]{:S(2)}, u32[]{:S(2)}) async-start(s32[8,1,64]{2,1,0:T(1,128)} %all_to_all.24), calls=%async_computation | async-start | bytes 8192 | tf_op jit(solution)/shard_map/all_to_all | solution.py:25
  18.8 4.3 %all-to-all-done = s32[8,1,64]{2,1,0:T(1,128)S(1)} async-done(((s32[8,1,64]{2,1,0:T(1,128)}), s32[8,1,64]{2,1,0:T(1,128)S(1)}, u32[]{:S(2)}, u32[]{:S(2)}) %all-to-all-start) | async-done | bytes 2080 | tf_op jit(solution)/shard_map/all_to_all | solution.py:25
  23.1 3.3 %all-to-all-start.1 = ((s32[8,1,64]{2,1,0:T(1,128)}), s32[8,1,64]{2,1,0:T(1,128)S(1)}, u32[]{:S(2)}, u32[]{:S(2)}) async-start(s32[8,1,64]{2,1,0:T(1,128)} %all_to_all.26), calls=%async_computation.1 | async-start | bytes 8192 | tf_op jit(solution)/shard_map/all_to_all | solution.py:26
  26.5 3.3 %scatter_custom_fusion = f32[4096]{0:T(1024)S(1)} fusion(s32[512]{0:T(512)S(1)} %bitcast.41, f32[512]{0:T(512)S(1)} %bitcast.36, f32[]{:T(128)} %constant.11.clone.1), kind=kCustom, calls=%fused_computation.40 | custom fusion | flops 512 | bytes 16388 | tf_op jit(solution)/shard_map/scatter-add | solution.py:16
  29.8 3.1 %gather_fusion = f32[512]{0:T(512)S(1)} fusion(f32[4096]{0:T(1024)S(1)} %rsqrt.3, s32[1024]{0:T(1024)S(1)} %pad_clamp_fusion.1), kind=kCustom, calls=%fused_computation | custom fusion | bytes 6144 | tf_op jit(solution)/shard_map/gather | solution.py:17
  34.4 3.3 %scatter_custom_fusion.1 = f32[2048]{0:T(1024)S(1)} fusion(s32[512]{0:T(512)S(1)} %reshape.181, f32[512]{0:T(512)S(1)} %reshape.183, f32[]{:T(128)} %constant.11.clone.1), kind=kCustom, calls=%fused_computation.45 | custom fusion | flops 512 | bytes 8196 | tf_op jit(solution)/shard_map/scatter-add | solution.py:29
  37.7 9.6 %all-gather.3.cloned.1.call-done = bf16[4096,512]{1,0:T(8,128)(2,1)} async-done(((bf16[4096,128]{1,0:T(8,128)(2,1)}), bf16[4096,512]{1,0:T(8,128)(2,1)}) %all-gather.3.cloned.1.call-update) | async-done | bytes 4194320 | tf_op jit(solution)/shard_map/all_gather | solution.py:18
  47.3 3.4 %convolution_convert_fusion.1 = bf16[4096,128]{1,0:T(8,128)(2,1)S(1)} fusion(bf16[4096,512]{1,0:T(8,128)(2,1)} %all-gather.3.cloned.1.call-done, bf16[512,128]{1,0:T(8,128)(2,1)S(1)} %copy-done.2), kind=kOutput, calls=%fused_computation.12 | convolution fusion | flops 537395200 | bytes 5373952 | tf_op jit(solution)/shard_map/dot_general | solution.py:19
  52.9 5.5 %all-to-all-start.2 = ((bf16[8,64,128]{2,1,0:T(8,128)(2,1)}), bf16[8,64,128]{2,1,0:T(8,128)(2,1)S(1)}, u32[]{:S(2)}, u32[]{:S(2)}) async-start(bf16[8,64,128]{2,1,0:T(8,128)(2,1)} %fusion.10), calls=%async_computation.2 | async-start | bytes 262144 | tf_op jit(solution)/shard_map/all_to_all | solution.py:22
  58.5 7.3 %all-to-all-done.2 = bf16[8,64,128]{2,1,0:T(8,128)(2,1)S(1)} async-done(((bf16[8,64,128]{2,1,0:T(8,128)(2,1)}), bf16[8,64,128]{2,1,0:T(8,128)(2,1)S(1)}, u32[]{:S(2)}, u32[]{:S(2)}) %all-to-all-start.2) | async-done | bytes 131104 | tf_op jit(solution)/shard_map/all_to_all | solution.py:22
  65.8 2.5 %scatter_custom_fusion.2 = f32[2048,128]{1,0:T(8,128)S(1)} fusion(s32[512]{0:T(512)S(1)} %reshape.181, f32[]{:T(128)} %constant.12.clone.1, bf16[512,128]{1,0:T(8,128)(2,1)S(1)} %bitcast.28), kind=kCustom, calls=%fused_computation.26 | custom fusion | flops 131072 | bytes 1179652 | tf_op jit(solution)/shard_map/scatter-add | solution.py:35
  68.7 1.3 gather_fusion.2
  70.1 9.9 %all_to_all.38 = bf16[8,64,128]{2,1,0:T(8,128)(2,1)S(1)} all-to-all(bf16[8,64,128]{2,1,0:T(8,128)(2,1)S(1)} %bitcast.33), channel_id=1, replica_groups=mesh['dom'=8,'feat'=4] {'dom'}, dimensions={0} | all-to-all | bytes 262144 | tf_op jit(solution)/shard_map/all_to_all | solution.py:45
  79.9 3.8 %scatter_custom_fusion.3 = f32[4096,128]{1,0:T(8,128)} fusion(s32[512]{0:T(512)S(1)} %bitcast.42, f32[]{:T(128)} %constant.12.clone.1, bf16[512,128]{1,0:T(8,128)(2,1)S(1)} %bitcast.34, f32[512]{0:T(512)S(1)} %bitcast.37), kind=kCustom, calls=%fused_computation.22 | custom fusion | flops 196608 | bytes 2230276 | tf_op jit(solution)/shard_map/scatter-add | solution.py:43
  83.7 3.2 %multiply_multiply_fusion = (f32[4096,128]{1,0:T(8,128)S(1)}, bf16[4096,128]{1,0:T(8,128)(2,1)}) fusion(bf16[4096,128]{1,0:T(8,128)(2,1)S(1)} %copy-done.1, f32[4096,128]{1,0:T(8,128)} %scatter_custom_fusion.3, f32[4096]{0:T(1024)S(1)} %rsqrt.3), kind=kLoop, calls=%fused_computation.14 | loop fusion | flops 6291456 | bytes 6307840 | tf_op jit(solution)/shard_map/mul | solution.py:50
  88.1 9.7 %all_to_all.39 = bf16[8,64,128]{2,1,0:T(8,128)(2,1)S(1)} all-to-all(bf16[8,64,128]{2,1,0:T(8,128)(2,1)S(1)} %multiply_convert_fusion.4), channel_id=1, replica_groups=mesh['dom'=8,'feat'=4] {'dom'}, dimensions={0} | all-to-all | bytes 262144 | tf_op jit(solution)/shard_map/all_to_all | solution.py:52
  97.8 2.5 %scatter_custom_fusion.4 = f32[2048,128]{1,0:T(8,128)S(1)} fusion(s32[512]{0:T(512)S(1)} %reshape.181, f32[]{:T(128)} %constant.12.clone.1, bf16[512,128]{1,0:T(8,128)(2,1)S(1)} %bitcast.30), kind=kCustom, calls=%fused_computation.24 | custom fusion | flops 131072 | bytes 1179652 | tf_op jit(solution)/shard_map/scatter-add | solution.py:35
  102.0 9.7 %all_to_all.40 = bf16[8,64,128]{2,1,0:T(8,128)(2,1)S(1)} all-to-all(bf16[8,64,128]{2,1,0:T(8,128)(2,1)S(1)} %bitcast.31), channel_id=1, replica_groups=mesh['dom'=8,'feat'=4] {'dom'}, dimensions={0} | all-to-all | bytes 262144 | tf_op jit(solution)/shard_map/all_to_all | solution.py:55
  111.7 2.9 %scatter_custom_fusion.5 = f32[4096,128]{1,0:T(8,128)S(1)} fusion(s32[512]{0:T(512)S(1)} %bitcast.43, f32[]{:T(128)} %constant.12.clone.1, bf16[512,128]{1,0:T(8,128)(2,1)S(1)} %bitcast.29, f32[512]{0:T(512)S(1)} %bitcast.38), kind=kCustom, calls=%fused_computation.20 | custom fusion | flops 196608 | bytes 2230276 | tf_op jit(solution)/shard_map/scatter-add | solution.py:43
  115.4 4.0 %convolution_bitcast_fusion = f32[512,128]{0,1:T(8,128)} fusion(bf16[4096,128]{1,0:T(8,128)(2,1)S(1)} %multiply_convert_fusion, bf16[4096,512]{1,0:T(8,128)(2,1)} %all-gather.3.cloned.1.call-done), kind=kOutput, calls=%fused_computation.17 | convolution fusion | flops 536870912 | bytes 5505024 | tf_op jit(solution)/shard_map/dot_general | solution.py:67
  120.2 6.5 %all_gather.11 = bf16[512,512]{1,0:T(8,128)(2,1)S(1)} all-gather(bf16[512,128]{1,0:T(8,128)(2,1)S(1)} %copy-done.2), channel_id=1, replica_groups=mesh['dom'=8,'feat'=4] {'feat'}, dimensions={1}, use_global_device_ids=true | all-gather | bytes 655360 | tf_op jit(solution)/shard_map/all_gather | solution.py:57
  126.7 60.2 %all-reduce.2.cloned.1.call-done = f32[512,128]{0,1:T(8,128)} async-done(((f32[512,128]{0,1:T(8,128)}), f32[512,128]{0,1:T(8,128)}) %all-reduce.2.cloned.1.call-update) | async-done | bytes 262160 | tf_op jit(solution)/shard_map/psum | solution.py:70
  188.6 34.9 %all-gather.5.cloned.1.call-done = bf16[4096,512]{1,0:T(8,128)(2,1)} async-done(((bf16[4096,128]{1,0:T(8,128)(2,1)}), bf16[4096,512]{1,0:T(8,128)(2,1)}) %all-gather.5.cloned.1.call-update) | async-done | bytes 4194320 | tf_op jit(solution)/shard_map/all_gather | solution.py:60
  223.5 4.4 %convolution_convert_fusion = bf16[4096,128]{1,0:T(8,128)(2,1)} fusion(bf16[4096,512]{1,0:T(8,128)(2,1)} %all-gather.5.cloned.1.call-done, bf16[512,512]{1,0:T(8,128)(2,1)S(1)} %all_gather.11, s32[]{:T(128)S(6)} %select_n.31), kind=kOutput, calls=%fused_computation.11 | convolution fusion | flops 537395200 | bytes 5373956 | tf_op jit(solution)/shard_map/dot_general | solution.py:59
  (44 shorter events, 14.4 us)
Async XLA Ops:
  7.2 30.6 %copy-start.3 = (f32[2048]{0:T(1024)S(1)}, f32[2048]{0:T(1024)}, u32[]{:S(2)}) copy-start(f32[2048]{0:T(1024)} %param.8) | copy-start | bytes 24580
  7.2 40.2 %copy-start.2 = (bf16[512,128]{1,0:T(8,128)(2,1)S(1)}, bf16[512,128]{1,0:T(8,128)(2,1)}, u32[]{:S(2)}) copy-start(bf16[512,128]{1,0:T(8,128)(2,1)} %param.6) | copy-start | bytes 393220
  7.2 40.1 %all-gather.3.cloned.1.call-start = ((), (), s32[]{:S(2)}) async-start(), calls=%async_computation.6 | async-start | bytes 5242880 | tf_op jit(solution)/shard_map/all_gather | solution.py:18
  9.4 13.7 %all-to-all-start = ((s32[8,1,64]{2,1,0:T(1,128)}), s32[8,1,64]{2,1,0:T(1,128)S(1)}, u32[]{:S(2)}, u32[]{:S(2)}) async-start(s32[8,1,64]{2,1,0:T(1,128)} %all_to_all.24), calls=%async_computation | async-start | bytes 8192 | tf_op jit(solution)/shard_map/all_to_all | solution.py:25
  23.1 11.3 %all-to-all-start.1 = ((s32[8,1,64]{2,1,0:T(1,128)}), s32[8,1,64]{2,1,0:T(1,128)S(1)}, u32[]{:S(2)}, u32[]{:S(2)}) async-start(s32[8,1,64]{2,1,0:T(1,128)} %all_to_all.26), calls=%async_computation.1 | async-start | bytes 8192 | tf_op jit(solution)/shard_map/all_to_all | solution.py:26
  52.9 12.9 %all-to-all-start.2 = ((bf16[8,64,128]{2,1,0:T(8,128)(2,1)}), bf16[8,64,128]{2,1,0:T(8,128)(2,1)S(1)}, u32[]{:S(2)}, u32[]{:S(2)}) async-start(bf16[8,64,128]{2,1,0:T(8,128)(2,1)} %fusion.10), calls=%async_computation.2 | async-start | bytes 262144 | tf_op jit(solution)/shard_map/all_to_all | solution.py:22
  58.4 128.5 %all-reduce.2.cloned.1.call-start = ((), (), s32[]{:S(2)}) async-start(), calls=%async_computation.8 | async-start | bytes 524288 | tf_op jit(solution)/shard_map/psum | solution.py:70
  68.7 15.0 %copy-start.1 = (bf16[4096,128]{1,0:T(8,128)(2,1)S(1)}, bf16[4096,128]{1,0:T(8,128)(2,1)}, u32[]{:S(2)}) copy-start(bf16[4096,128]{1,0:T(8,128)(2,1)} %param.9) | copy-start | bytes 3145732
  115.4 4.1 %copy-start = (bf16[4096,128]{1,0:T(8,128)(2,1)}, bf16[4096,128]{1,0:T(8,128)(2,1)S(1)}, u32[]{:S(2)}) copy-start(bf16[4096,128]{1,0:T(8,128)(2,1)S(1)} %multiply_convert_fusion) | copy-start | bytes 3145732
  119.4 104.1 %all-gather.5.cloned.1.call-start = ((), (), s32[]{:S(2)}) async-start(), calls=%async_computation.7 | async-start | bytes 5242880 | tf_op jit(solution)/shard_map/all_gather | solution.py:60
Sparse Core Ops, SparseCore 0:
  9.6 37.7 all-gather.2
  119.6 67.3 all-reduce.1
  189.2 34.2 all-gather.4
where the time goes:
time: 235 us; the launch traced here: 234 us
  waiting for transfers between devices  118 us (50%)
  blocking collectives  35.9 us (15%)
  other arithmetic  26.6 us (11%)
  starting transfers between devices  16.2 us (7%)
  between operations  14 us (6%)
  local copies, waits for them, and re-layouts  12.1 us (5%)
  matrix products  11.9 us (5%)
    psum x1, waiting for transfers between devices, local(): total = lax.psum(term, 'dom')  60.2 us
    all_gather x1, waiting for transfers between devices, local(): lax.all_gather(grad_projected, 'feat', axis=1, tiled=True)  34.9 us
    all_to_all x1, blocking collectives, local(): lax.all_to_all(edge_side(recv_rows), 'dom', split_axis=0, concat_axis=0,...  9.85 us
    all_to_all x1, blocking collectives, local(): lax.all_to_all(grad_message.reshape(owners, -1, cols), 'dom', split_axis=...  9.74 us
    all_to_all x1, blocking collectives, local(): lax.all_to_all(edge_side(grad_recv), 'dom', split_axis=0, concat_axis=0,...  9.74 us
    all_gather x1, waiting for transfers between devices, local(): full_rows = lax.all_gather(features, 'feat', axis=1, tiled=True)  9.59 us
    all_to_all x1, waiting for transfers between devices, local(): lax.all_to_all(message.reshape(owners, -1, cols), 'dom', split_axis=0, co...  7.34 us
    all_to_all x1, starting transfers between devices, local(): lax.all_to_all(edge.reshape(owners, -1), 'dom', split_axis=0, concat_axis...  7.28 us
  transfers between devices with their start and end apart: 6, of which 5 were waited for; matrix products, arithmetic and copies ran while one was open for 6% of the time, Pallas kernels for 0%

commit v1 on v0

--- a/solution.py
+++ b/solution.py
@@ -67,7 +67,7 @@
     term = lax.dot_general(
         full_rows, grad_projected, (((0,), (0,)), ((), ())), preferred_element_type=jnp.float32
     )
-    total = lax.psum(term, "dom")
+    total = jnp.sum(lax.all_gather(term, "dom"), axis=0)
     grad_theta = lax.dynamic_slice_in_dim(total, lax.axis_index("dom") * share, share, 0)
     return (activation, grad_features, grad_theta)
 

time: 235 us -> 213 us (0.906)
  waiting for transfers between devices: 118 us -> 92.7 us
  local copies, waits for them, and re-layouts: 12.1 us -> 14.5 us
    psum x1 -> x0, waiting for transfers between devices: 60.2 us -> none  [local(): total = lax.psum(term, 'dom')]
    all_gather x0 -> x1, waiting for transfers between devices: none -> 39 us  [local(): total = jnp.sum(lax.all_gather(term, 'dom'), axis=0)]
    all_gather x1, waiting for transfers between devices: 34.9 us -> 31.1 us  [local(): lax.all_gather(grad_projected, 'feat', axis=1, tiled=True)]
    unnamed x9 -> x10, local copies, waits for them, and re-layouts: 0.73 us -> 3.95 us
  transfers between devices with their start and end apart: 6 -> 6, of which waited for: 5 -> 5; matrix products, arithmetic and copies ran while one was open for 6% -> 8% of each run, Pallas kernels for 0% -> 0%
where the time goes in v1:
time: 213 us; the launch traced here: 212 us
  waiting for transfers between devices  92.7 us (44%)
  blocking collectives  35.9 us (17%)
  other arithmetic  27.1 us (13%)
  starting transfers between devices  16.2 us (8%)
  local copies, waits for them, and re-layouts  14.5 us (7%)
  between operations  14 us (7%)
  matrix products  11.9 us (6%)
    all_gather x1, waiting for transfers between devices, local(): total = jnp.sum(lax.all_gather(term, 'dom'), axis=0)  39 us
    all_gather x1, waiting for transfers between devices, local(): lax.all_gather(grad_projected, 'feat', axis=1, tiled=True)  31.1 us
    all_to_all x1, blocking collectives, local(): lax.all_to_all(edge_side(recv_rows), 'dom', split_axis=0, concat_axis=0,...  9.85 us
    all_to_all x1, blocking collectives, local(): lax.all_to_all(grad_message.reshape(owners, -1, cols), 'dom', split_axis=...  9.74 us
    all_to_all x1, blocking collectives, local(): lax.all_to_all(edge_side(grad_recv), 'dom', split_axis=0, concat_axis=0,...  9.74 us
    all_gather x1, waiting for transfers between devices, local(): full_rows = lax.all_gather(features, 'feat', axis=1, tiled=True)  9.58 us
    all_to_all x1, waiting for transfers between devices, local(): lax.all_to_all(message.reshape(owners, -1, cols), 'dom', split_axis=0, co...  7.34 us
    all_to_all x1, starting transfers between devices, local(): lax.all_to_all(edge.reshape(owners, -1), 'dom', split_axis=0, concat_axis...  7.28 us
  transfers between devices with their start and end apart: 6, of which 5 were waited for; matrix products, arithmetic and copies ran while one was open for 8% of the time, Pallas kernels for 0%

profile of v1, /device:TPU:0, one launch (start us, length us, event | category | flops | bytes accessed | tf_op | source)
XLA Modules:
  0.0 212.3 jit_solution(587673213727598264)
XLA Ops:
  9.4 7.3 %all-to-all-start = ((s32[8,1,64]{2,1,0:T(1,128)}), s32[8,1,64]{2,1,0:T(1,128)S(1)}, u32[]{:S(2)}, u32[]{:S(2)}) async-start(s32[8,1,64]{2,1,0:T(1,128)} %all_to_all.24), calls=%async_computation | async-start | bytes 8192 | tf_op jit(solution)/shard_map/all_to_all | solution.py:25
  18.8 4.3 %all-to-all-done = s32[8,1,64]{2,1,0:T(1,128)S(1)} async-done(((s32[8,1,64]{2,1,0:T(1,128)}), s32[8,1,64]{2,1,0:T(1,128)S(1)}, u32[]{:S(2)}, u32[]{:S(2)}) %all-to-all-start) | async-done | bytes 2080 | tf_op jit(solution)/shard_map/all_to_all | solution.py:25
  23.1 3.3 %all-to-all-start.1 = ((s32[8,1,64]{2,1,0:T(1,128)}), s32[8,1,64]{2,1,0:T(1,128)S(1)}, u32[]{:S(2)}, u32[]{:S(2)}) async-start(s32[8,1,64]{2,1,0:T(1,128)} %all_to_all.26), calls=%async_computation.1 | async-start | bytes 8192 | tf_op jit(solution)/shard_map/all_to_all | solution.py:26
  26.4 3.3 %scatter_custom_fusion = f32[4096]{0:T(1024)S(1)} fusion(s32[512]{0:T(512)S(1)} %bitcast.47, f32[512]{0:T(512)S(1)} %bitcast.42, f32[]{:T(128)} %constant.11.clone.1), kind=kCustom, calls=%fused_computation.41 | custom fusion | flops 512 | bytes 16388 | tf_op jit(solution)/shard_map/scatter-add | solution.py:16
  29.7 3.1 %gather_fusion = f32[512]{0:T(512)S(1)} fusion(f32[4096]{0:T(1024)S(1)} %rsqrt.3, s32[1024]{0:T(1024)S(1)} %pad_clamp_fusion.1), kind=kCustom, calls=%fused_computation | custom fusion | bytes 6144 | tf_op jit(solution)/shard_map/gather | solution.py:17
  34.5 3.3 %scatter_custom_fusion.1 = f32[2048]{0:T(1024)S(1)} fusion(s32[512]{0:T(512)S(1)} %reshape.181, f32[512]{0:T(512)S(1)} %reshape.183, f32[]{:T(128)} %constant.11.clone.1), kind=kCustom, calls=%fused_computation.46 | custom fusion | flops 512 | bytes 8196 | tf_op jit(solution)/shard_map/scatter-add | solution.py:29
  37.7 9.6 %all-gather.5.cloned.1.call-done = bf16[4096,512]{1,0:T(8,128)(2,1)} async-done(((bf16[4096,128]{1,0:T(8,128)(2,1)}), bf16[4096,512]{1,0:T(8,128)(2,1)}) %all-gather.5.cloned.1.call-update) | async-done | bytes 4194320 | tf_op jit(solution)/shard_map/all_gather | solution.py:18
  47.3 3.4 %convolution_convert_fusion.1 = bf16[4096,128]{1,0:T(8,128)(2,1)S(1)} fusion(bf16[4096,512]{1,0:T(8,128)(2,1)} %all-gather.5.cloned.1.call-done, bf16[512,128]{1,0:T(8,128)(2,1)S(1)} %copy-done.2), kind=kOutput, calls=%fused_computation.12 | convolution fusion | flops 537395200 | bytes 5373952 | tf_op jit(solution)/shard_map/dot_general | solution.py:19
  52.9 5.5 %all-to-all-start.2 = ((bf16[8,64,128]{2,1,0:T(8,128)(2,1)}), bf16[8,64,128]{2,1,0:T(8,128)(2,1)S(1)}, u32[]{:S(2)}, u32[]{:S(2)}) async-start(bf16[8,64,128]{2,1,0:T(8,128)(2,1)} %fusion.10), calls=%async_computation.2 | async-start | bytes 262144 | tf_op jit(solution)/shard_map/all_to_all | solution.py:22
  58.5 7.3 %all-to-all-done.2 = bf16[8,64,128]{2,1,0:T(8,128)(2,1)S(1)} async-done(((bf16[8,64,128]{2,1,0:T(8,128)(2,1)}), bf16[8,64,128]{2,1,0:T(8,128)(2,1)S(1)}, u32[]{:S(2)}, u32[]{:S(2)}) %all-to-all-start.2) | async-done | bytes 131104 | tf_op jit(solution)/shard_map/all_to_all | solution.py:22
  65.8 2.5 %scatter_custom_fusion.2 = f32[2048,128]{1,0:T(8,128)S(1)} fusion(s32[512]{0:T(512)S(1)} %reshape.181, f32[]{:T(128)} %constant.12.clone.1, bf16[512,128]{1,0:T(8,128)(2,1)S(1)} %bitcast.34), kind=kCustom, calls=%fused_computation.27 | custom fusion | flops 131072 | bytes 1179652 | tf_op jit(solution)/shard_map/scatter-add | solution.py:35
  70.1 9.9 %all_to_all.38 = bf16[8,64,128]{2,1,0:T(8,128)(2,1)S(1)} all-to-all(bf16[8,64,128]{2,1,0:T(8,128)(2,1)S(1)} %bitcast.39), channel_id=1, replica_groups=mesh['dom'=8,'feat'=4] {'dom'}, dimensions={0} | all-to-all | bytes 262144 | tf_op jit(solution)/shard_map/all_to_all | solution.py:45
  79.9 3.8 %scatter_custom_fusion.3 = f32[4096,128]{1,0:T(8,128)} fusion(s32[512]{0:T(512)S(1)} %bitcast.48, f32[]{:T(128)} %constant.12.clone.1, bf16[512,128]{1,0:T(8,128)(2,1)S(1)} %bitcast.40, f32[512]{0:T(512)S(1)} %bitcast.43), kind=kCustom, calls=%fused_computation.23 | custom fusion | flops 196608 | bytes 2230276 | tf_op jit(solution)/shard_map/scatter-add | solution.py:43
  83.7 3.1 %multiply_multiply_fusion = (f32[4096,128]{1,0:T(8,128)S(1)}, bf16[4096,128]{1,0:T(8,128)(2,1)}) fusion(bf16[4096,128]{1,0:T(8,128)(2,1)S(1)} %copy-done.1, f32[4096,128]{1,0:T(8,128)} %scatter_custom_fusion.3, f32[4096]{0:T(1024)S(1)} %rsqrt.3), kind=kLoop, calls=%fused_computation.15 | loop fusion | flops 6291456 | bytes 6307840 | tf_op jit(solution)/shard_map/mul | solution.py:50
  88.0 9.7 %all_to_all.39 = bf16[8,64,128]{2,1,0:T(8,128)(2,1)S(1)} all-to-all(bf16[8,64,128]{2,1,0:T(8,128)(2,1)S(1)} %multiply_convert_fusion.4), channel_id=1, replica_groups=mesh['dom'=8,'feat'=4] {'dom'}, dimensions={0} | all-to-all | bytes 262144 | tf_op jit(solution)/shard_map/all_to_all | solution.py:52
  97.8 2.5 %scatter_custom_fusion.4 = f32[2048,128]{1,0:T(8,128)S(1)} fusion(s32[512]{0:T(512)S(1)} %reshape.181, f32[]{:T(128)} %constant.12.clone.1, bf16[512,128]{1,0:T(8,128)(2,1)S(1)} %bitcast.36), kind=kCustom, calls=%fused_computation.25 | custom fusion | flops 131072 | bytes 1179652 | tf_op jit(solution)/shard_map/scatter-add | solution.py:35
  102.0 9.7 %all_to_all.40 = bf16[8,64,128]{2,1,0:T(8,128)(2,1)S(1)} all-to-all(bf16[8,64,128]{2,1,0:T(8,128)(2,1)S(1)} %bitcast.37), channel_id=1, replica_groups=mesh['dom'=8,'feat'=4] {'dom'}, dimensions={0} | all-to-all | bytes 262144 | tf_op jit(solution)/shard_map/all_to_all | solution.py:55
  111.7 2.9 %scatter_custom_fusion.5 = f32[4096,128]{1,0:T(8,128)S(1)} fusion(s32[512]{0:T(512)S(1)} %bitcast.49, f32[]{:T(128)} %constant.12.clone.1, bf16[512,128]{1,0:T(8,128)(2,1)S(1)} %bitcast.35, f32[512]{0:T(512)S(1)} %bitcast.44), kind=kCustom, calls=%fused_computation.21 | custom fusion | flops 196608 | bytes 2230276 | tf_op jit(solution)/shard_map/scatter-add | solution.py:43
  115.3 4.0 %convolution_bitcast_fusion = f32[512,128]{0,1:T(8,128)} fusion(bf16[4096,128]{1,0:T(8,128)(2,1)S(1)} %multiply_convert_fusion, bf16[4096,512]{1,0:T(8,128)(2,1)} %all-gather.5.cloned.1.call-done), kind=kOutput, calls=%fused_computation.18 | convolution fusion | flops 536870912 | bytes 5505024 | tf_op jit(solution)/shard_map/dot_general | solution.py:67
  120.1 6.5 %all_gather.17 = bf16[512,512]{1,0:T(8,128)(2,1)S(1)} all-gather(bf16[512,128]{1,0:T(8,128)(2,1)S(1)} %copy-done.2), channel_id=1, replica_groups=mesh['dom'=8,'feat'=4] {'feat'}, dimensions={1}, use_global_device_ids=true | all-gather | bytes 655360 | tf_op jit(solution)/shard_map/all_gather | solution.py:57
  126.7 39.0 %all-gather.9.cloned.1.call-done = f32[4096,128]{0,1:T(8,128)} async-done(((f32[512,128]{0,1:T(8,128)}), f32[4096,128]{0,1:T(8,128)}) %all-gather.9.cloned.1.call-update) | async-done | bytes 2097168 | tf_op jit(solution)/shard_map/all_gather | solution.py:70
  165.7 3.2 %copy.9 = f32[16,8,8,512]{3,2,1,0:T(8,128)S(1)} copy(f32[16,8,8,512]{3,1,2,0:T(8,128)} %bitcast.32) | data formatting | bytes 4194304
  170.2 31.1 %all-gather.7.cloned.1.call-done = bf16[4096,512]{1,0:T(8,128)(2,1)} async-done(((bf16[4096,128]{1,0:T(8,128)(2,1)}), bf16[4096,512]{1,0:T(8,128)(2,1)}) %all-gather.7.cloned.1.call-update) | async-done | bytes 4194320 | tf_op jit(solution)/shard_map/all_gather | solution.py:60
  201.3 4.4 %convolution_convert_fusion = bf16[4096,128]{1,0:T(8,128)(2,1)} fusion(bf16[4096,512]{1,0:T(8,128)(2,1)} %all-gather.7.cloned.1.call-done, bf16[512,512]{1,0:T(8,128)(2,1)S(1)} %all_gather.17, s32[]{:T(128)S(6)} %select_n.31), kind=kOutput, calls=%fused_computation.11 | convolution fusion | flops 537395200 | bytes 5373956 | tf_op jit(solution)/shard_map/dot_general | solution.py:59
  (46 shorter events, 15.4 us)
Async XLA Ops:
  7.2 30.6 %copy-start.3 = (f32[2048]{0:T(1024)S(1)}, f32[2048]{0:T(1024)}, u32[]{:S(2)}) copy-start(f32[2048]{0:T(1024)} %param.8) | copy-start | bytes 24580
  7.2 40.2 %copy-start.2 = (bf16[512,128]{1,0:T(8,128)(2,1)S(1)}, bf16[512,128]{1,0:T(8,128)(2,1)}, u32[]{:S(2)}) copy-start(bf16[512,128]{1,0:T(8,128)(2,1)} %param.6) | copy-start | bytes 393220
  7.2 40.1 %all-gather.5.cloned.1.call-start = ((), (), s32[]{:S(2)}) async-start(), calls=%async_computation.6 | async-start | bytes 5242880 | tf_op jit(solution)/shard_map/all_gather | solution.py:18
  9.4 13.7 %all-to-all-start = ((s32[8,1,64]{2,1,0:T(1,128)}), s32[8,1,64]{2,1,0:T(1,128)S(1)}, u32[]{:S(2)}, u32[]{:S(2)}) async-start(s32[8,1,64]{2,1,0:T(1,128)} %all_to_all.24), calls=%async_computation | async-start | bytes 8192 | tf_op jit(solution)/shard_map/all_to_all | solution.py:25
  23.1 11.2 %all-to-all-start.1 = ((s32[8,1,64]{2,1,0:T(1,128)}), s32[8,1,64]{2,1,0:T(1,128)S(1)}, u32[]{:S(2)}, u32[]{:S(2)}) async-start(s32[8,1,64]{2,1,0:T(1,128)} %all_to_all.26), calls=%async_computation.1 | async-start | bytes 8192 | tf_op jit(solution)/shard_map/all_to_all | solution.py:26
  52.9 12.9 %all-to-all-start.2 = ((bf16[8,64,128]{2,1,0:T(8,128)(2,1)}), bf16[8,64,128]{2,1,0:T(8,128)(2,1)S(1)}, u32[]{:S(2)}, u32[]{:S(2)}) async-start(bf16[8,64,128]{2,1,0:T(8,128)(2,1)} %fusion.10), calls=%async_computation.2 | async-start | bytes 262144 | tf_op jit(solution)/shard_map/all_to_all | solution.py:22
  58.4 107.2 %all-gather.9.cloned.1.call-start = ((), (), s32[]{:S(2)}) async-start(), calls=%async_computation.8 | async-start | bytes 2359296 | tf_op jit(solution)/shard_map/all_gather | solution.py:70
  68.7 15.0 %copy-start.1 = (bf16[4096,128]{1,0:T(8,128)(2,1)S(1)}, bf16[4096,128]{1,0:T(8,128)(2,1)}, u32[]{:S(2)}) copy-start(bf16[4096,128]{1,0:T(8,128)(2,1)} %param.9) | copy-start | bytes 3145732
  115.3 4.0 %copy-start = (bf16[4096,128]{1,0:T(8,128)(2,1)}, bf16[4096,128]{1,0:T(8,128)(2,1)S(1)}, u32[]{:S(2)}) copy-start(bf16[4096,128]{1,0:T(8,128)(2,1)S(1)} %multiply_convert_fusion) | copy-start | bytes 3145732
  119.4 81.9 %all-gather.7.cloned.1.call-start = ((), (), s32[]{:S(2)}) async-start(), calls=%async_computation.7 | async-start | bytes 5242880 | tf_op jit(solution)/shard_map/all_gather | solution.py:60
Sparse Core Ops, SparseCore 0:
  9.6 37.7 all-gather.4
  119.5 46.0 all-gather.8
  167.8 33.4 all-gather.6
